TPU v7x, 32 devices: a whole 2x2x4 slice. The times are simulated.
32 devices in a mesh: sub: 8 (over z, x), row: 4 (over y, core).
Axes of the slice: x: 2, y: 2, z: 4, core: 2. Of those that a mesh axis runs over, the one named last changes fastest.
Arguments:
- residual: float32 [32, 8, 2048], P(None, 'sub', 'row')
- factor: float32 [8, 3072, 3072], P('sub', 'row'), may hold values from -0.0390625 to 0.0390625
- basis: float32 [96, 8, 2048], P(None, 'sub', 'row'), may hold values from -0.046875 to 0.046875
- send_rows: int32 [8, 2, 512], P('sub'), may hold values from 0 to 2047, as said below
Outputs:
- coeffs: float32 [96, 32], replicated
- rfactor: float32 [32, 32], replicated
- block_q: float32 [32, 8, 2048], P(None, 'sub', 'row')
Inputs may be any that keep to these rules, and one draw needn't show every extreme that they name: Within each send_rows[s, side, :] the rows are distinct.
All inputs are finite; a program needn't handle non-finite values.
Results may differ from a plain program's by a relative error of at most 0.000073.
Values sent between devices are 32-bit elements; how exact they have to be, the bound alone decides.
A program may use at most 64 MiB of HBM per device.

v0:
```python
import jax
import jax.numpy as jnp
from jax import lax
from jax.sharding import PartitionSpec as P

HIGH = lax.Precision.HIGHEST


def from_behind(value, axis, steps):
    count = lax.axis_size(axis)
    leading, last = (max(0, -steps), min(count, count - steps))
    return lax.ppermute(value, axis, [(source, source + steps) for source in range(leading, last)])


def contract_rows(left_mat, right_mat):
    return lax.dot_general(left_mat, right_mat, (((1,), (1,)), ((), ())), precision=HIGH)


def contract_first(left_mat, right_mat):
    return lax.dot_general(left_mat, right_mat, (((0,), (0,)), ((), ())), precision=HIGH)


def second_sum(inner):
    return lax.psum(inner, ("sub", "row"))


def per_device(residual, factor, basis, send_rows):
    slab = residual.shape[2]
    row_count = lax.axis_size("row")
    sub_rows = slab * row_count
    total_rows = sub_rows * lax.axis_size("sub")
    own_rows = residual[:, 0, :]
    whole = lax.all_gather(own_rows, "row", axis=1, tiled=True)
    index_rows = send_rows[0]
    to_lower = jnp.take(whole, index_rows[0], axis=1)
    to_upper = jnp.take(whole, index_rows[1], axis=1)
    from_lower = from_behind(to_upper, "sub", 1)
    from_upper = from_behind(to_lower, "sub", -1)
    extended = jnp.concatenate([whole, from_lower, from_upper], axis=1)
    factor_rows = factor[0]
    share = factor_rows.shape[0]
    margin = from_lower.shape[1]
    row_pos = lax.axis_index("row")
    global_rows = row_pos * share + lax.iota(jnp.int32, share)
    columns = lax.iota(jnp.int32, factor_rows.shape[1])
    full = factor_rows + (global_rows[:, None] == columns[None, :]).astype(jnp.float32)
    inner = contract_rows(extended, full)
    partial_value = jnp.dot(inner, full, precision=HIGH)
    summed = lax.psum(partial_value, "row")
    mine = lax.dynamic_slice_in_dim(summed, row_pos * slab, slab, 1)
    margins = summed[:, sub_rows:]
    back_upper = from_behind(margins[:, :margin], "sub", -1)
    back_lower = from_behind(margins[:, margin:], "sub", 1)
    my_rows = row_pos * slab + lax.iota(jnp.int32, slab)
    select_upper = (index_rows[1][:, None] == my_rows[None, :]).astype(jnp.float32)
    select_lower = (index_rows[0][:, None] == my_rows[None, :]).astype(jnp.float32)
    block_t = (
        mine
        + jnp.dot(back_upper, select_upper, precision=HIGH)
        + jnp.dot(back_lower, select_lower, precision=HIGH)
    )
    vectors = basis[:, 0, :]
    first = lax.psum(contract_rows(vectors, block_t), ("sub", "row"))
    once = block_t - contract_first(first, vectors)
    inner_two = contract_rows(vectors, once)
    second = second_sum(inner_two)
    twice = once - contract_first(second, vectors)
    gram = lax.psum(contract_rows(twice, twice), ("sub", "row")) / total_rows
    lower_tri = jnp.linalg.cholesky(gram)
    solved = jax.scipy.linalg.solve_triangular(lower_tri, twice, lower=True)
    return (first + second, lower_tri.T, solved[:, None, :])


def solution(mesh):
    placed = (
        P(None, "sub", "row"),
        P("sub", "row", None),
        P(None, "sub", "row"),
        P("sub", None, None),
    )
    return jax.shard_map(
        per_device,
        mesh=mesh,
        in_specs=placed,
        out_specs=(P(), P(), P(None, "sub", "row")),
        check_vma=False,
    )
```

profile of v0, /device:TPU:0, one launch (start us, length us, event | category | flops | bytes accessed | tf_op | source)
XLA Modules:
  0.0 240.3 jit_solution(11160368016298102574)
XLA Ops:
  7.2 0.8 fusion.30
  8.0 1.0 copy.12
  9.0 11.5 %all-gather = f32[32,1,2048]{0,2,1:T(8,128)S(1)} all-gather(f32[32,1,512]{0,2,1:T(8,128)S(1)} %copy.12), channel_id=2, replica_groups=mesh['sub'=8,'row'=4] {'row'}, dimensions={2}, use_global_device_ids=true | all-gather | bytes 327680 | tf_op jit(solution)/shard_map/all_gather | solution.py:33
  20.5 1.0 gather_fusion
  21.7 3.4 %collective-permute-start = (f32[32,512]{0,1:T(8,128)S(1)}, f32[32,512]{0,1:T(8,128)S(1)}, u32[]{:S(2)}, u32[]{:S(2)}) collective-permute-start(f32[32,512]{0,1:T(8,128)S(1)} %select_bitcast_fusion.1), channel_id=1, source_target_pairs={{0,4},{4,8},{8,12},{12,16},{16,20},{20,24},{24,28},{1,5},{5,9},{9,... | collective-permute-start | bytes 196616 | tf_op jit(solution)/shard_map/ppermute | solution.py:12
  25.1 1.0 gather_fusion.1
  26.3 1.3 collective-permute-start.1
  27.6 0.3 copy.13
  27.9 8.9 %collective-permute-done = f32[32,512]{0,1:T(8,128)S(1)} collective-permute-done((f32[32,512]{0,1:T(8,128)S(1)}, f32[32,512]{0,1:T(8,128)S(1)}, u32[]{:S(2)}, u32[]{:S(2)}) %collective-permute-start) | collective-permute-done | bytes 65568 | tf_op jit(solution)/shard_map/ppermute | solution.py:12
  37.0 11.7 %fusion.1 = f32[32,768]{1,0:T(8,128)S(1)} fusion(f32[1,768,3072]{2,1,0:T(8,128)} %param.7, s32[768]{0:T(1024)S(1)} %iota_add_fusion, f32[32,512]{1,0:T(8,128)S(1)} %copy.15, f32[32,512]{1,0:T(8,128)S(1)} %copy.14, f32[32,2048]{1,0:T(8,128)S(1)} %copy.13), kind=kOutput, calls=%fused_computation.5 | convolution fusion | flops 913244160 | bytes 9931776 | tf_op jit(solution)/shard_map/dot_general | solution.py:16
  48.8 7.4 %fusion = f32[32,3072]{1,0:T(8,128)} fusion(f32[32,768]{1,0:T(8,128)S(1)} %fusion.1, f32[1,768,3072]{2,1,0:T(8,128)S(1)} %copy-done, s32[768]{0:T(1024)S(1)} %iota_add_fusion), kind=kOutput, calls=%fused_computation.4 | convolution fusion | flops 913047552 | bytes 9931776 | tf_op jit(solution)/shard_map/dot_general | solution.py:48
  56.2 34.4 %all-reduce.2.cloned.1.call-done = f32[32,3072]{1,0:T(8,128)} async-done(((f32[32,3072]{1,0:T(8,128)}), f32[32,3072]{1,0:T(8,128)}) %all-reduce.2.cloned.1.call-update) | async-done | bytes 393232 | tf_op jit(solution)/shard_map/psum | solution.py:49
  90.6 0.9 fusion.29
  91.5 3.4 %collective-permute-start.3 = (f32[32,512]{1,0:T(8,128)S(1)}, f32[32,512]{1,0:T(8,128)S(1)}, u32[]{:S(2)}, u32[]{:S(2)}) collective-permute-start(f32[32,512]{1,0:T(8,128)S(1)} %get-tuple-element.11), channel_id=1, source_target_pairs={{0,4},{4,8},{8,12},{12,16},{16,20},{20,24},{24,28},{1,5},{5,9},{9,... | collective-permute-start | bytes 196616 | tf_op jit(solution)/shard_map/ppermute | solution.py:12
  94.9 1.5 collective-permute-start.2
  96.4 0.4 collective-permute-done.3
  96.8 0.5 fusion.5
  97.3 3.8 %collective-permute-done.2 = f32[32,512]{1,0:T(8,128)S(1)} collective-permute-done((f32[32,512]{1,0:T(8,128)S(1)}, f32[32,512]{1,0:T(8,128)S(1)}, u32[]{:S(2)}, u32[]{:S(2)}) %collective-permute-start.2) | collective-permute-done | bytes 65568 | tf_op jit(solution)/shard_map/ppermute | solution.py:12
  101.1 1.4 fusion.4
  102.4 0.3 convolution_bitcast_fusion.2
  102.8 40.3 %psum.29 = f32[96,32]{0,1:T(8,128)S(1)} all-reduce(f32[96,32]{0,1:T(8,128)S(1)} %convolution_bitcast_fusion.2), channel_id=1, replica_groups=mesh['sub'=8,'row'=4] {'sub','row'}, use_global_device_ids=true, to_apply=%region_1.3 | all-reduce | flops 3072 | bytes 24576 | tf_op jit(solution)/shard_map/psum | solution.py:63
  143.3 0.3 convolution_bitcast_fusion.1
  143.6 40.1 %psum.30 = f32[96,32]{0,1:T(8,128)S(1)} all-reduce(f32[96,32]{0,1:T(8,128)S(1)} %convolution_bitcast_fusion.1), channel_id=1, replica_groups=mesh['sub'=8,'row'=4] {'sub','row'}, use_global_device_ids=true, to_apply=%region_2.4 | all-reduce | flops 3072 | bytes 24576 | tf_op jit(solution)/shard_map/psum | solution.py:24
  183.9 0.6 add.69
  184.7 40.3 %psum.31 = f32[32,32]{0,1:T(8,128)S(1)} all-reduce(f32[32,32]{0,1:T(8,128)S(1)} %fusion.31), channel_id=1, replica_groups=mesh['sub'=8,'row'=4] {'sub','row'}, use_global_device_ids=true, to_apply=%region_3.5 | all-reduce | flops 1024 | bytes 8192 | tf_op jit(solution)/shard_map/psum | solution.py:68
  225.1 2.9 %cholesky.18 = f32[32,32]{1,0:T(8,128)S(1)} custom-call(f32[32,32]{1,0:T(8,128)S(1)} %fusion.26), custom_call_target="Cholesky" | custom-call | tf_op jit(solution)/shard_map/jit(cholesky)/cholesky | solution.py:69
  228.1 0.6 compare_reduce_fusion
  228.7 0.7 select_bitcast_fusion.2
  229.4 2.4 %custom-call.7 = f32[1,32,32]{1,2,0:T(8,128)S(1)} custom-call(f32[1,32,32]{2,1,0:T(8,128)S(1)} %get-tuple-element.12), custom_call_target="InvertDiagBlocksLowerTriangular" | custom-call | tf_op jit(solution)/shard_map/jit(_solve_triangular)/triangular_solve | solution.py:70
  231.8 0.3 convolution_bitcast_fusion
  232.1 0.7 copy.19
  232.8 0.7 copy.18
  (26 shorter events, 1.3 us)
Async XLA Ops:
  7.2 83.4 %all-reduce.2.cloned.1.call-start = ((), (), s32[]{:S(2)}) async-start(), calls=%async_computation | async-start | bytes 786432 | tf_op jit(solution)/shard_map/psum | solution.py:49
  21.7 15.1 %collective-permute-start = (f32[32,512]{0,1:T(8,128)S(1)}, f32[32,512]{0,1:T(8,128)S(1)}, u32[]{:S(2)}, u32[]{:S(2)}) collective-permute-start(f32[32,512]{0,1:T(8,128)S(1)} %select_bitcast_fusion.1), channel_id=1, source_target_pairs={{0,4},{4,8},{8,12},{12,16},{16,20},{20,24},{24,28},{1,5},{5,9},{9,... | collective-permute-start | bytes 196616 | tf_op jit(solution)/shard_map/ppermute | solution.py:12
  26.3 10.6 %collective-permute-start.1 = (f32[32,512]{0,1:T(8,128)S(1)}, f32[32,512]{0,1:T(8,128)S(1)}, u32[]{:S(2)}, u32[]{:S(2)}) collective-permute-start(f32[32,512]{0,1:T(8,128)S(1)} %select_bitcast_fusion), channel_id=1, source_target_pairs={{4,0},{8,4},{12,8},{16,12},{20,16},{24,20},{28,24},{5,1},{9,5},{13... | collective-permute-start | bytes 196616 | tf_op jit(solution)/shard_map/ppermute | solution.py:12
  37.0 11.8 %copy-start = (f32[1,768,3072]{2,1,0:T(8,128)S(1)}, f32[1,768,3072]{2,1,0:T(8,128)}, u32[]{:S(2)}) copy-start(f32[1,768,3072]{2,1,0:T(8,128)} %param.7) | copy-start | bytes 28311556
  37.0 65.4 %copy-start.1 = (f32[96,1,512]{2,1,0:T(1,128)S(1)}, f32[96,1,512]{2,1,0:T(1,128)}, u32[]{:S(2)}) copy-start(f32[96,1,512]{2,1,0:T(1,128)} %param.8) | copy-start | bytes 589828
  91.5 5.3 %collective-permute-start.3 = (f32[32,512]{1,0:T(8,128)S(1)}, f32[32,512]{1,0:T(8,128)S(1)}, u32[]{:S(2)}, u32[]{:S(2)}) collective-permute-start(f32[32,512]{1,0:T(8,128)S(1)} %get-tuple-element.11), channel_id=1, source_target_pairs={{0,4},{4,8},{8,12},{12,16},{16,20},{20,24},{24,28},{1,5},{5,9},{9,... | collective-permute-start | bytes 196616 | tf_op jit(solution)/shard_map/ppermute | solution.py:12
  94.9 6.2 %collective-permute-start.2 = (f32[32,512]{1,0:T(8,128)S(1)}, f32[32,512]{1,0:T(8,128)S(1)}, u32[]{:S(2)}, u32[]{:S(2)}) collective-permute-start(f32[32,512]{1,0:T(8,128)S(1)} %get-tuple-element.10), channel_id=1, source_target_pairs={{4,0},{8,4},{12,8},{16,12},{20,16},{24,20},{28,24},{5,1},{9,5},{13... | collective-permute-start | bytes 196616 | tf_op jit(solution)/shard_map/ppermute | solution.py:12
Sparse Core Ops, SparseCore 0:
  56.3 34.2 all-reduce.1
where the time goes:
time: 241 us; the launch traced here: 240 us
  blocking collectives  132 us (55%)
  waiting for transfers between devices  47.5 us (20%)
  matrix products  22.6 us (9%)
  between operations  14.3 us (6%)
  starting transfers between devices  9.59 us (4%)
  other arithmetic  7.62 us (3%)
  local copies, waits for them, and re-layouts  6.65 us (3%)
    psum x1, blocking collectives, per_device(): first = lax.psum(contract_rows(vectors, block_t), ('sub', 'row'))  40.3 us
    psum x1, blocking collectives, per_device(): gram = lax.psum(contract_rows(twice, twice), ('sub', 'row')) / total_rows  40.3 us
    psum x1, blocking collectives, second_sum(): return lax.psum(inner, ('sub', 'row'))  40.1 us
    psum x1, waiting for transfers between devices, per_device(): summed = lax.psum(partial_value, 'row')  34.4 us
    ppermute x4, waiting for transfers between devices, from_behind(): lax.ppermute(value, axis, [(source, source + steps) for source in range(l...  13 us
    dot_general x4, matrix products, contract_rows(): lax.dot_general(left_mat, right_mat, (((1,), (1,)), ((), ())), precision=...  12.6 us
    all_gather x1, blocking collectives, per_device(): whole = lax.all_gather(own_rows, 'row', axis=1, tiled=True)  11.5 us
    ppermute x4, starting transfers between devices, from_behind(): lax.ppermute(value, axis, [(source, source + steps) for source in range(l...  9.55 us
  transfers between devices with their start and end apart: 5, of which 4 were waited for; matrix products, arithmetic and copies ran while one was open for 1% of the time, Pallas kernels for 0%

commit v1 on v0

v1 whole, which is shorter than its diff:
```python
import functools

import jax
import jax.numpy as jnp
from jax import lax
from jax.experimental import pallas as pl
from jax.experimental.pallas import tpu as pltpu
from jax.sharding import PartitionSpec as P

HIGH = lax.Precision.HIGHEST
MESH = pl.DeviceIdType.MESH
F32 = jnp.float32
BF16 = jnp.bfloat16
LOADS = 6


def dot_nt(left, right, precision=None):
    return lax.dot_general(
        left, right, (((1,), (1,)), ((), ())), precision=precision, preferred_element_type=F32
    )


def dot_nn(left, right, precision=None):
    return lax.dot_general(
        left, right, (((1,), (0,)), ((), ())), precision=precision, preferred_element_type=F32
    )


def split_two(value):
    high = value.astype(BF16)
    return high, (value - high.astype(F32)).astype(BF16)


def split_three(value):
    high = value.astype(BF16)
    rest = value - high.astype(F32)
    mid = rest.astype(BF16)
    return high, mid, (rest - mid.astype(F32)).astype(BF16)


def factor_gram(gram, vecs):
    eye = (
        lax.broadcasted_iota(jnp.int32, (vecs, vecs), 0)
        == lax.broadcasted_iota(jnp.int32, (vecs, vecs), 1)
    ).astype(F32)
    work = jnp.concatenate([gram, eye, jnp.zeros((vecs, 128 - 2 * vecs), F32)], axis=1)
    row_of = lax.broadcasted_iota(jnp.int32, (vecs, 1), 0)
    for step in range(vecs - 1):
        scale = 1.0 / work[step : step + 1, step : step + 1]
        multiplier = jnp.where(row_of > step, work[:, step : step + 1] * scale, 0.0)
        work = work - multiplier * work[step : step + 1, :]
    rows = lax.broadcasted_iota(jnp.int32, work.shape, 0)
    lanes = lax.broadcasted_iota(jnp.int32, work.shape, 1)
    pivots = jnp.sum(jnp.where(rows == lanes, work, 0.0), axis=1, keepdims=True)
    work = jnp.where(lanes >= rows, work, 0.0) * (1.0 / jnp.sqrt(pivots))
    return work[:, :vecs], work[:, vecs : 2 * vecs]


def kernel(
    subs,
    rows_n,
    res_ref,
    fac_ref,
    bas_ref,
    idx_ref,
    coef_ref,
    rfac_ref,
    q_ref,
    fac,
    fhi,
    flo,
    ext,
    stack,
    sel,
    acc,
    part,
    rs_own,
    rs_mar,
    back_q,
    back,
    hot,
    vpad,
    g_part,
    g_rs,
    g_sub,
    g_full,
    f_row,
    f_sub,
    c_row,
    c_sub,
    load_sem,
    row_send,
    row_recv,
    near_send,
    near_recv,
    sub_send,
    sub_recv,
):
    sub = lax.axis_index("sub")
    row = lax.axis_index("row")
    vecs, slab = res_ref.shape
    share, wide = fac_ref.shape
    nb = bas_ref.shape[0]
    margin = idx_ref.shape[1]
    own = slab * rows_n
    quarter = margin // rows_n
    total_rows = own * subs
    has_lower = sub > 0
    has_upper = sub < subs - 1
    started = []

    def row_peer(k):
        return lax.rem(row + k, rows_n)

    def sub_peer(k):
        return lax.rem(sub + k, subs)

    load_rows = share // LOADS
    loads = []
    for i in range(LOADS):
        span = pl.ds(i * load_rows, load_rows)
        loads.append(pltpu.make_async_copy(fac_ref.at[span], fac.at[span], load_sem.at[i]))
        loads[-1].start()

    barrier = pltpu.get_barrier_semaphore()

    def greet(to_sub, to_row):
        pl.semaphore_signal(barrier, inc=1, device_id=(to_sub, to_row), device_id_type=MESH)

    for k in range(1, rows_n):
        greet(sub, row_peer(k))

    @pl.when(has_lower)
    def _():
        for k in range(1, rows_n):
            greet(sub - 1, row_peer(k))

    @pl.when(has_upper)
    def _():
        for k in range(1, rows_n):
            greet(sub + 1, row_peer(k))

    for k in range(1, subs):
        greet(sub_peer(k), row)
    near = has_lower.astype(jnp.int32) + has_upper.astype(jnp.int32)
    ext[:, pl.ds(pl.multiple_of(row * slab, 128), slab)] = res_ref[...]
    pl.semaphore_wait(barrier, (rows_n - 1) * (1 + near) + subs - 1)

    def row_copies(slot, source_of, target_of):
        copies = []
        for k in range(1, rows_n):
            peer = row_peer(k)
            copies.append(
                pltpu.make_async_remote_copy(
                    source_of(peer),
                    target_of(k),
                    row_send.at[slot, k - 1],
                    row_recv.at[slot, k - 1],
                    device_id=(sub, peer),
                    device_id_type=MESH,
                )
            )
            copies[-1].start()
        started.extend(copies)
        return copies

    def sub_copies(slot, ref):
        copies = []
        for k in range(1, subs):
            copies.append(
                pltpu.make_async_remote_copy(
                    ref.at[sub],
                    ref.at[sub],
                    sub_send.at[slot, k - 1],
                    sub_recv.at[slot, k - 1],
                    device_id=(sub_peer(k), row),
                    device_id_type=MESH,
                )
            )
            copies[-1].start()
        started.extend(copies)
        return copies

    def near_copies(slot, up, source, target):
        to_sub = sub + 1 if up else sub - 1
        return [
            pltpu.make_async_remote_copy(
                source,
                target,
                near_send.at[slot, k],
                near_recv.at[slot, k],
                device_id=(to_sub, row_peer(k)),
                device_id_type=MESH,
            )
            for k in range(rows_n)
        ]

    def near_start(up, copies):
        @pl.when(has_upper if up else has_lower)
        def _():
            for copy in copies:
                copy.start()

    def near_wait(up, copies):
        @pl.when(has_lower if up else has_upper)
        def _():
            for copy in copies:
                copy.wait_recv()

    def near_finish(up, copies):
        @pl.when(has_upper if up else has_lower)
        def _():
            for copy in copies:
                copy.wait_send()

    def landed(copies):
        for copy in copies:
            copy.wait_recv()

    slab_copies = row_copies(
        0,
        lambda peer: res_ref,
        lambda k: ext.at[:, pl.ds(pl.multiple_of(row * slab, 128), slab)],
    )

    vpad[:nb] = bas_ref[...]
    vpad[nb:] = jnp.zeros((vpad.shape[0] - nb, slab), F32)
    g_part[...] = dot_nt(vpad[...], vpad[...], HIGH)
    g_rows = nb // rows_n

    def g_span(which):
        return pl.ds(pl.multiple_of(which * g_rows, 8), g_rows)

    g_copies = row_copies(1, lambda peer: g_part.at[g_span(peer)], lambda k: g_rs.at[k - 1])

    for i in range(LOADS):
        loads[i].wait()

        @pl.loop(0, load_rows // 16)
        def _(j):
            span = pl.ds(pl.multiple_of(i * load_rows + j * 16, 16), 16)
            high, low = split_two(fac[span, :])
            fhi[span, :] = high
            flo[span, :] = low

    base = lax.broadcasted_iota(jnp.int32, (own, quarter), 0)
    picks = []
    for side in range(2):
        index = idx_ref[side : side + 1, pl.ds(pl.multiple_of(row * quarter, 128), quarter)]
        picks.append((base == index).astype(F32).astype(BF16))
    pick = jnp.concatenate(picks, axis=1)
    landed(slab_copies)
    whole = ext[:, :own]
    pieces = jnp.concatenate(split_three(whole), axis=0)
    chosen = dot_nn(pieces, pick)
    chosen = chosen[:vecs] + chosen[vecs : 2 * vecs] + chosen[2 * vecs :]
    sel[0] = chosen[:, :quarter]
    sel[1] = chosen[:, quarter:]

    def ext_span(side):
        return ext.at[:, pl.ds(pl.multiple_of(own + side * margin + row * quarter, 128), quarter)]

    up_copies = near_copies(0, True, sel.at[1], ext_span(0))
    down_copies = near_copies(1, False, sel.at[0], ext_span(1))
    near_start(True, up_copies)
    near_start(False, down_copies)

    @pl.when(jnp.logical_not(has_lower))
    def _():
        ext[:, own : own + margin] = jnp.zeros((vecs, margin), F32)

    @pl.when(jnp.logical_not(has_upper))
    def _():
        ext[:, own + margin :] = jnp.zeros((vecs, margin), F32)

    landed(g_copies)
    g_mine = g_part[g_span(row), :]
    for k in range(1, rows_n):
        g_mine = g_mine + g_rs[k - 1]
    g_sub[sub] = g_mine
    g_across = sub_copies(0, g_sub)

    high, low = split_two(whole)
    stack[:vecs, :own] = high
    stack[vecs:, :own] = low
    step = 256

    def first_product(lo, hi, add):
        for j in range(0, share, step):
            both = dot_nt(stack[:, lo:hi], fhi[j : j + step, lo:hi])
            value = both[:vecs] + both[vecs:] + dot_nt(stack[:vecs, lo:hi], flo[j : j + step, lo:hi])
            acc[:, j : j + step] = acc[:, j : j + step] + value if add else value

    first_product(0, own, False)
    my_rows = row * slab + lax.broadcasted_iota(jnp.int32, (slab, margin), 0)
    hot[:, :margin] = (my_rows == idx_ref[1:2, :]).astype(F32).astype(BF16)
    hot[:, margin:] = (my_rows == idx_ref[0:1, :]).astype(F32).astype(BF16)
    near_wait(True, up_copies)
    near_wait(False, down_copies)
    high, low = split_two(ext[:, own:])
    stack[:vecs, own:] = high
    stack[vecs:, own:] = low
    first_product(own, wide, True)
    mine_cols = pl.ds(pl.multiple_of(row * share, 128), share)
    inner = acc[...] + ext[:, mine_cols]
    part[...] = jnp.zeros((vecs, wide), F32)
    part[:, mine_cols] = inner

    landed(g_across)
    g_sum = g_sub[0]
    for k in range(1, subs):
        g_sum = g_sum + g_sub[k]
    g_full[g_span(row), :] = g_sum
    g_full[nb:, :] = jnp.zeros((g_full.shape[0] - nb, g_full.shape[1]), F32)
    g_gather = row_copies(
        2, lambda peer: g_full.at[g_span(row)], lambda k: g_full.at[g_span(row)]
    )

    high, low = split_two(inner)
    both_in = jnp.concatenate([high, low], axis=0)

    def second_product(lo):
        both = dot_nn(both_in, fhi[:, lo : lo + slab])
        value = both[:vecs] + both[vecs:] + dot_nn(high, flo[:, lo : lo + slab])
        part[:, lo : lo + slab] = part[:, lo : lo + slab] + value

    for lo in range(own, wide, slab):
        second_product(lo)

    def margin_of(side, which):
        return part.at[:, pl.ds(pl.multiple_of(own + side * margin + which * quarter, 128), quarter)]

    mar0 = row_copies(3, lambda peer: margin_of(0, peer), lambda k: rs_mar.at[k - 1, 0])
    mar1 = row_copies(4, lambda peer: margin_of(1, peer), lambda k: rs_mar.at[k - 1, 1])
    for lo in range(0, own, slab):
        second_product(lo)

    def own_of(which):
        return part.at[:, pl.ds(pl.multiple_of(which * slab, 128), slab)]

    own_copies = row_copies(5, own_of, lambda k: rs_own.at[k - 1])
    landed(mar0)
    landed(mar1)
    for side in range(2):
        total = margin_of(side, row)[...]
        for k in range(1, rows_n):
            total = total + rs_mar[k - 1, side]
        back_q[side] = total

    def back_span(side):
        return back.at[:, pl.ds(pl.multiple_of(side * margin + row * quarter, 128), quarter)]

    back_down = near_copies(2, False, back_q.at[0], back_span(0))
    back_up = near_copies(3, True, back_q.at[1], back_span(1))
    near_start(False, back_down)
    near_start(True, back_up)

    @pl.when(jnp.logical_not(has_upper))
    def _():
        back[:, :margin] = jnp.zeros((vecs, margin), F32)

    @pl.when(jnp.logical_not(has_lower))
    def _():
        back[:, margin:] = jnp.zeros((vecs, margin), F32)

    landed(own_copies)
    block_t = own_of(row)[...]
    for k in range(1, rows_n):
        block_t = block_t + rs_own[k - 1]
    landed(g_gather)
    near_wait(False, back_down)
    near_wait(True, back_up)
    added = dot_nt(jnp.concatenate(split_three(back[...]), axis=0), hot[...])
    block_t = block_t + (added[:vecs] + added[vecs : 2 * vecs] + added[2 * vecs :])

    def sum_all(value, slot, row_slot, by_row, by_sub):
        by_row[row] = value
        landed(row_copies(row_slot, lambda peer: by_row.at[row], lambda k: by_row.at[row]))
        total = by_row[0]
        for k in range(1, rows_n):
            total = total + by_row[k]
        by_sub[sub] = total
        landed(sub_copies(slot, by_sub))
        total = by_sub[0]
        for k in range(1, subs):
            total = total + by_sub[k]
        return total

    first = sum_all(dot_nt(block_t, vpad[...], HIGH), 1, 6, f_row, f_sub)
    second = first - dot_nn(first, g_full[...], HIGH)
    coeffs = first + second
    twice = block_t - dot_nn(coeffs, vpad[...], HIGH)
    gram = dot_nt(twice, twice, HIGH)
    fold = 128 // vecs
    tall = vecs // fold
    packed = jnp.concatenate([gram[i * tall : (i + 1) * tall] for i in range(fold)], axis=1)
    coef_ref[...] = coeffs.T[:nb]
    packed = sum_all(packed, 2, 7, c_row, c_sub) * (1.0 / total_rows)
    gram = jnp.concatenate([packed[:, i * vecs : (i + 1) * vecs] for i in range(fold)], axis=0)
    upper, inverse = factor_gram(gram, vecs)
    rfac_ref[...] = upper
    q_ref[...] = dot_nn(inverse, twice, HIGH)

    for copy in started:
        copy.wait_send()
    near_finish(True, up_copies)
    near_finish(False, down_copies)
    near_finish(False, back_down)
    near_finish(True, back_up)


def per_device(residual, factor, basis, send_rows):
    subs = lax.axis_size("sub")
    rows_n = lax.axis_size("row")
    vecs, _, slab = residual.shape
    nb = basis.shape[0]
    _, share, wide = factor.shape
    margin = send_rows.shape[2]
    quarter = margin // rows_n
    pad = -(-nb // 128) * 128
    g_rows = nb // rows_n
    fold = 128 // vecs
    vmem = pl.BlockSpec(memory_space=pltpu.VMEM)
    coeffs, rfactor, block_q = pl.pallas_call(
        functools.partial(kernel, subs, rows_n),
        out_shape=(
            jax.ShapeDtypeStruct((nb, vecs), F32),
            jax.ShapeDtypeStruct((vecs, vecs), F32),
            jax.ShapeDtypeStruct((vecs, slab), F32),
        ),
        in_specs=[vmem, pl.BlockSpec(memory_space=pl.ANY), vmem, vmem],
        out_specs=(vmem, vmem, vmem),
        scratch_shapes=[
            pltpu.VMEM((share, wide), F32),
            pltpu.VMEM((share, wide), BF16),
            pltpu.VMEM((share, wide), BF16),
            pltpu.VMEM((vecs, wide), F32),
            pltpu.VMEM((2 * vecs, wide), BF16),
            pltpu.VMEM((2, vecs, quarter), F32),
            pltpu.VMEM((vecs, share), F32),
            pltpu.VMEM((vecs, wide), F32),
            pltpu.VMEM((rows_n - 1, vecs, slab), F32),
            pltpu.VMEM((rows_n - 1, 2, vecs, quarter), F32),
            pltpu.VMEM((2, vecs, quarter), F32),
            pltpu.VMEM((vecs, 2 * margin), F32),
            pltpu.VMEM((slab, 2 * margin), BF16),
            pltpu.VMEM((pad, slab), F32),
            pltpu.VMEM((pad, pad), F32),
            pltpu.VMEM((rows_n - 1, g_rows, pad), F32),
            pltpu.VMEM((subs, g_rows, pad), F32),
            pltpu.VMEM((pad, pad), F32),
            pltpu.VMEM((rows_n, vecs, pad), F32),
            pltpu.VMEM((subs, vecs, pad), F32),
            pltpu.VMEM((rows_n, vecs // fold, 128), F32),
            pltpu.VMEM((subs, vecs // fold, 128), F32),
            pltpu.SemaphoreType.DMA((LOADS,)),
            pltpu.SemaphoreType.DMA((8, rows_n - 1)),
            pltpu.SemaphoreType.DMA((8, rows_n - 1)),
            pltpu.SemaphoreType.DMA((4, rows_n)),
            pltpu.SemaphoreType.DMA((4, rows_n)),
            pltpu.SemaphoreType.DMA((3, subs - 1)),
            pltpu.SemaphoreType.DMA((3, subs - 1)),
        ],
        compiler_params=pltpu.CompilerParams(
            collective_id=0, has_side_effects=True, vmem_limit_bytes=40 * 1024 * 1024
        ),
        cost_estimate=pl.CostEstimate(
            flops=12 * vecs * share * wide, bytes_accessed=4 * share * wide, transcendentals=0
        ),
    )(residual[:, 0, :], factor[0], basis[:, 0, :], send_rows[0])
    return coeffs, rfactor, block_q[:, None, :]


def solution(mesh):
    placed = (
        P(None, "sub", "row"),
        P("sub", "row", None),
        P(None, "sub", "row"),
        P("sub", None, None),
    )
    return jax.shard_map(
        per_device,
        mesh=mesh,
        in_specs=placed,
        out_specs=(P(), P(), P(None, "sub", "row")),
        check_vma=False,
    )
```

time: 241 us -> 57.1 us (0.24)
  blocking collectives: 132 us -> 0 us
  Pallas kernels: 0 us -> 48 us
  waiting for transfers between devices: 47.5 us -> 0 us
  matrix products: 22.6 us -> 0 us
  between operations: 14.3 us -> 0.65 us
  starting transfers between devices: 9.59 us -> 0 us
  other arithmetic: 7.62 us -> 0 us
    psum x3 -> x0, blocking collectives: 121 us -> none  [the longest x1 40.3 us: per_device(): first = lax.psum(contract_rows(vectors, block_t), ('sub', 'row'))]
    pallas_call x0 -> x1, Pallas kernels: none -> 48 us  [per_device(): pl.pallas_call(functools.partial(kernel, subs, rows_n), out_shape=(jax.Sh...]
    psum x1 -> x0, waiting for transfers between devices: 34.4 us -> none  [per_device(): summed = lax.psum(partial_value, 'row')]
    dot_general x9 -> x0, matrix products: 22.3 us -> none  [the longest x4 12.6 us: contract_rows(): lax.dot_general(left_mat, right_mat, (((1,), (1,)), ((), ())), precision=...]
    ppermute x4 -> x0, waiting for transfers between devices: 13 us -> none  [from_behind(): lax.ppermute(value, axis, [(source, source + steps) for source in range(l...]
    all_gather x1 -> x0, blocking collectives: 11.5 us -> none  [per_device(): whole = lax.all_gather(own_rows, 'row', axis=1, tiled=True)]
    ppermute x4 -> x0, starting transfers between devices: 9.55 us -> none  [from_behind(): lax.ppermute(value, axis, [(source, source + steps) for source in range(l...]
    another operation x5 -> x0, other arithmetic: 6.68 us -> none  [the longest x3 3.6 us: per_device(): lower_tri = jnp.linalg.cholesky(gram)]
  transfers between devices with their start and end apart: 5 -> 0, of which waited for: 4 -> 0; matrix products, arithmetic and copies ran while one was open for 1% -> 0% of each run, Pallas kernels for 0% -> 0%
where the time goes in v1:
time: 57.1 us; the launch traced here: 56.8 us
  Pallas kernels  48 us (84%)
  local copies, waits for them, and re-layouts  8.13 us (14%)
  between operations  0.65 us (1%)
    pallas_call x1, Pallas kernels, per_device(): pl.pallas_call(functools.partial(kernel, subs, rows_n), out_shape=(jax.Sh...  48 us
    unnamed x9, local copies, waits for them, and re-layouts  8.13 us

profile of v1, /device:TPU:0, one launch (start us, length us, event | category | flops | bytes accessed | tf_op | source)
XLA Modules:
  0.0 56.8 jit_solution(11073003182014373765)
XLA Ops:
  0.6 0.8 %copy.14 = f32[32,1,512]{2,0,1:T(8,128)S(1)} copy(f32[32,1,512]{2,1,0:T(1,128)} %param.4) | data formatting | bytes 131072
  1.5 0.9 %copy.13 = f32[96,1,512]{2,0,1:T(8,128)S(1)} copy(f32[96,1,512]{2,1,0:T(1,128)} %param.6) | data formatting | bytes 393216
  2.4 0.0 copy-start
  2.4 3.7 %copy-done = f32[1,768,3072]{2,1,0:T(8,128)S(1)} copy-done((f32[1,768,3072]{2,1,0:T(8,128)S(1)}, f32[1,768,3072]{2,1,0:T(8,128)}, u32[]{:S(2)}) %copy-start) | copy-done | bytes 9437208
  6.1 0.0 copy-start.1
  6.1 0.7 %copy-done.1 = s32[1,2,512]{2,1,0:T(2,128)S(1)} copy-done((s32[1,2,512]{2,1,0:T(2,128)S(1)}, s32[1,2,512]{2,1,0:T(2,128)}, u32[]{:S(2)}) %copy-start.1) | copy-done | bytes 4120
  6.8 48.0 %shard_map.67 = (f32[96,32]{1,0:T(8,128)S(1)}, f32[32,32]{1,0:T(8,128)S(1)}, f32[32,512]{1,0:T(8,128)S(1)}) custom-call(f32[32,512]{1,0:T(8,128)S(1)} %bitcast.11, f32[768,3072]{1,0:T(8,128)S(1)} %bitcast.9, f32[96,512]{1,0:T(8,128)S(1)} %bitcast.10, s32[2,512]{1,0:T(2,128)S(1)} %bitcast.13), custom_call_target="tpu_custom_call" | custom-call | flops 905969664 | bytes 9437184 | tf_op jit(solution)/shard_map/pallas_call | solution.py:424
  54.8 0.7 %copy.7 = f32[96,32]{0,1:T(8,128)} copy(f32[96,32]{1,0:T(8,128)S(1)} %get-tuple-element.9) | data formatting | bytes 24576
  55.5 0.7 %copy.8 = f32[32,1,512]{2,1,0:T(1,128)} copy(f32[32,1,512]{2,0,1:T(8,128)S(1)} %bitcast.12) | data formatting | bytes 131072
  56.2 0.6 %copy.16 = f32[32,32]{1,0:T(8,128)} copy(f32[32,32]{1,0:T(8,128)S(1)} %get-tuple-element.16) | data formatting | bytes 8192
Async XLA Ops:
  2.4 3.7 %copy-start = (f32[1,768,3072]{2,1,0:T(8,128)S(1)}, f32[1,768,3072]{2,1,0:T(8,128)}, u32[]{:S(2)}) copy-start(f32[1,768,3072]{2,1,0:T(8,128)} %param.5) | copy-start | bytes 28311556
  6.1 0.7 %copy-start.1 = (s32[1,2,512]{2,1,0:T(2,128)S(1)}, s32[1,2,512]{2,1,0:T(2,128)}, u32[]{:S(2)}) copy-start(s32[1,2,512]{2,1,0:T(2,128)} %param.7) | copy-start | bytes 12292

commit v2 on v1

--- a/solution.py
+++ b/solution.py
@@ -59,13 +59,16 @@
 def kernel(
     subs,
     rows_n,
+    res_hbm,
+    fac_hbm,
+    bas_hbm,
+    idx_hbm,
+    coef_ref,
+    gram_ref,
+    twice_ref,
     res_ref,
-    fac_ref,
     bas_ref,
     idx_ref,
-    coef_ref,
-    rfac_ref,
-    q_ref,
     fac,
     fhi,
     flo,
@@ -88,6 +91,9 @@
     f_sub,
     c_row,
     c_sub,
+    f_part,
+    c_full,
+    small_sem,
     load_sem,
     row_send,
     row_recv,
@@ -98,8 +104,8 @@
 ):
     sub = lax.axis_index("sub")
     row = lax.axis_index("row")
-    vecs, slab = res_ref.shape
-    share, wide = fac_ref.shape
+    vecs, _, slab = res_ref.shape
+    share, wide = fac.shape
     nb = bas_ref.shape[0]
     margin = idx_ref.shape[1]
     own = slab * rows_n
@@ -115,11 +121,19 @@
     def sub_peer(k):
         return lax.rem(sub + k, subs)
 
+    small = [
+        pltpu.make_async_copy(source, target, small_sem.at[i])
+        for i, (source, target) in enumerate(
+            [(res_hbm, res_ref), (idx_hbm.at[0], idx_ref), (bas_hbm, bas_ref)]
+        )
+    ]
+    for copy in small:
+        copy.start()
     load_rows = share // LOADS
     loads = []
     for i in range(LOADS):
         span = pl.ds(i * load_rows, load_rows)
-        loads.append(pltpu.make_async_copy(fac_ref.at[span], fac.at[span], load_sem.at[i]))
+        loads.append(pltpu.make_async_copy(fac_hbm.at[0, span], fac.at[span], load_sem.at[i]))
         loads[-1].start()
 
     barrier = pltpu.get_barrier_semaphore()
@@ -143,7 +157,9 @@
     for k in range(1, subs):
         greet(sub_peer(k), row)
     near = has_lower.astype(jnp.int32) + has_upper.astype(jnp.int32)
-    ext[:, pl.ds(pl.multiple_of(row * slab, 128), slab)] = res_ref[...]
+    own_slab = ext.at[:, pl.ds(pl.multiple_of(row * slab, 128), slab)]
+    small[0].wait()
+    own_slab[...] = res_ref[:, 0, :]
     pl.semaphore_wait(barrier, (rows_n - 1) * (1 + near) + subs - 1)
 
     def row_copies(slot, source_of, target_of):
@@ -217,38 +233,17 @@
         for copy in copies:
             copy.wait_recv()
 
-    slab_copies = row_copies(
-        0,
-        lambda peer: res_ref,
-        lambda k: ext.at[:, pl.ds(pl.multiple_of(row * slab, 128), slab)],
-    )
-
-    vpad[:nb] = bas_ref[...]
-    vpad[nb:] = jnp.zeros((vpad.shape[0] - nb, slab), F32)
-    g_part[...] = dot_nt(vpad[...], vpad[...], HIGH)
-    g_rows = nb // rows_n
-
-    def g_span(which):
-        return pl.ds(pl.multiple_of(which * g_rows, 8), g_rows)
-
-    g_copies = row_copies(1, lambda peer: g_part.at[g_span(peer)], lambda k: g_rs.at[k - 1])
-
-    for i in range(LOADS):
-        loads[i].wait()
-
-        @pl.loop(0, load_rows // 16)
-        def _(j):
-            span = pl.ds(pl.multiple_of(i * load_rows + j * 16, 16), 16)
-            high, low = split_two(fac[span, :])
-            fhi[span, :] = high
-            flo[span, :] = low
-
+    slab_copies = row_copies(0, lambda peer: own_slab, lambda k: own_slab)
+    small[1].wait()
     base = lax.broadcasted_iota(jnp.int32, (own, quarter), 0)
     picks = []
     for side in range(2):
         index = idx_ref[side : side + 1, pl.ds(pl.multiple_of(row * quarter, 128), quarter)]
         picks.append((base == index).astype(F32).astype(BF16))
     pick = jnp.concatenate(picks, axis=1)
+    small[2].wait()
+    vpad[:nb] = bas_ref[:, 0, :]
+    vpad[nb:] = jnp.zeros((vpad.shape[0] - nb, slab), F32)
     landed(slab_copies)
     whole = ext[:, :own]
     pieces = jnp.concatenate(split_three(whole), axis=0)
@@ -273,6 +268,36 @@
     def _():
         ext[:, own + margin :] = jnp.zeros((vecs, margin), F32)
 
+    g_part[...] = dot_nt(vpad[...], vpad[...], HIGH)
+    g_rows = nb // rows_n
+
+    def g_span(which):
+        return pl.ds(pl.multiple_of(which * g_rows, 8), g_rows)
+
+    g_copies = row_copies(1, lambda peer: g_part.at[g_span(peer)], lambda k: g_rs.at[k - 1])
+
+    for i in range(LOADS):
+        loads[i].wait()
+
+        @pl.loop(0, load_rows // 16)
+        def _(j):
+            span = pl.ds(pl.multiple_of(i * load_rows + j * 16, 16), 16)
+            high, low = split_two(fac[span, :])
+            fhi[span, :] = high
+            flo[span, :] = low
+
+    high, low = split_two(whole)
+    stack[:vecs, :own] = high
+    stack[vecs:, :own] = low
+    step = 256
+
+    def first_product(lo, hi, add):
+        for j in range(0, share, step):
+            both = dot_nt(stack[:, lo:hi], fhi[j : j + step, lo:hi])
+            value = both[:vecs] + both[vecs:] + dot_nt(stack[:vecs, lo:hi], flo[j : j + step, lo:hi])
+            acc[:, j : j + step] = acc[:, j : j + step] + value if add else value
+
+    first_product(0, own, False)
     landed(g_copies)
     g_mine = g_part[g_span(row), :]
     for k in range(1, rows_n):
@@ -280,21 +305,6 @@
     g_sub[sub] = g_mine
     g_across = sub_copies(0, g_sub)
 
-    high, low = split_two(whole)
-    stack[:vecs, :own] = high
-    stack[vecs:, :own] = low
-    step = 256
-
-    def first_product(lo, hi, add):
-        for j in range(0, share, step):
-            both = dot_nt(stack[:, lo:hi], fhi[j : j + step, lo:hi])
-            value = both[:vecs] + both[vecs:] + dot_nt(stack[:vecs, lo:hi], flo[j : j + step, lo:hi])
-            acc[:, j : j + step] = acc[:, j : j + step] + value if add else value
-
-    first_product(0, own, False)
-    my_rows = row * slab + lax.broadcasted_iota(jnp.int32, (slab, margin), 0)
-    hot[:, :margin] = (my_rows == idx_ref[1:2, :]).astype(F32).astype(BF16)
-    hot[:, margin:] = (my_rows == idx_ref[0:1, :]).astype(F32).astype(BF16)
     near_wait(True, up_copies)
     near_wait(False, down_copies)
     high, low = split_two(ext[:, own:])
@@ -306,6 +316,29 @@
     part[...] = jnp.zeros((vecs, wide), F32)
     part[:, mine_cols] = inner
 
+    high, low = split_two(inner)
+    both_in = jnp.concatenate([high, low], axis=0)
+
+    def second_product(lo):
+        both = dot_nn(both_in, fhi[:, lo : lo + slab])
+        value = both[:vecs] + both[vecs:] + dot_nn(high, flo[:, lo : lo + slab])
+        part[:, lo : lo + slab] = part[:, lo : lo + slab] + value
+
+    for lo in range(own, wide, slab):
+        second_product(lo)
+
+    def margin_of(side, which):
+        return part.at[:, pl.ds(pl.multiple_of(own + side * margin + which * quarter, 128), quarter)]
+
+    mar0 = row_copies(3, lambda peer: margin_of(0, peer), lambda k: rs_mar.at[k - 1, 0])
+    mar1 = row_copies(4, lambda peer: margin_of(1, peer), lambda k: rs_mar.at[k - 1, 1])
+    for lo in range(0, own, slab):
+        second_product(lo)
+
+    def own_of(which):
+        return part.at[:, pl.ds(pl.multiple_of(which * slab, 128), slab)]
+
+    own_copies = row_copies(5, own_of, lambda k: rs_own.at[k - 1])
     landed(g_across)
     g_sum = g_sub[0]
     for k in range(1, subs):
@@ -315,30 +348,6 @@
     g_gather = row_copies(
         2, lambda peer: g_full.at[g_span(row)], lambda k: g_full.at[g_span(row)]
     )
-
-    high, low = split_two(inner)
-    both_in = jnp.concatenate([high, low], axis=0)
-
-    def second_product(lo):
-        both = dot_nn(both_in, fhi[:, lo : lo + slab])
-        value = both[:vecs] + both[vecs:] + dot_nn(high, flo[:, lo : lo + slab])
-        part[:, lo : lo + slab] = part[:, lo : lo + slab] + value
-
-    for lo in range(own, wide, slab):
-        second_product(lo)
-
-    def margin_of(side, which):
-        return part.at[:, pl.ds(pl.multiple_of(own + side * margin + which * quarter, 128), quarter)]
-
-    mar0 = row_copies(3, lambda peer: margin_of(0, peer), lambda k: rs_mar.at[k - 1, 0])
-    mar1 = row_copies(4, lambda peer: margin_of(1, peer), lambda k: rs_mar.at[k - 1, 1])
-    for lo in range(0, own, slab):
-        second_product(lo)
-
-    def own_of(which):
-        return part.at[:, pl.ds(pl.multiple_of(which * slab, 128), slab)]
-
-    own_copies = row_copies(5, own_of, lambda k: rs_own.at[k - 1])
     landed(mar0)
     landed(mar1)
     for side in range(2):
@@ -363,11 +372,13 @@
     def _():
         back[:, margin:] = jnp.zeros((vecs, margin), F32)
 
+    my_rows = row * slab + lax.broadcasted_iota(jnp.int32, (slab, margin), 0)
+    hot[:, :margin] = (my_rows == idx_ref[1:2, :]).astype(F32).astype(BF16)
+    hot[:, margin:] = (my_rows == idx_ref[0:1, :]).astype(F32).astype(BF16)
     landed(own_copies)
     block_t = own_of(row)[...]
     for k in range(1, rows_n):
         block_t = block_t + rs_own[k - 1]
-    landed(g_gather)
     near_wait(False, back_down)
     near_wait(True, back_up)
     added = dot_nt(jnp.concatenate(split_three(back[...]), axis=0), hot[...])
@@ -386,20 +397,34 @@
             total = total + by_sub[k]
         return total
 
-    first = sum_all(dot_nt(block_t, vpad[...], HIGH), 1, 6, f_row, f_sub)
+    eighth = vecs // rows_n
+
+    def vec_span(which):
+        return pl.ds(pl.multiple_of(which * eighth, 8), eighth)
+
+    f_part[...] = dot_nt(block_t, vpad[...], HIGH)
+    landed(row_copies(6, lambda peer: f_part.at[vec_span(peer)], lambda k: f_row.at[k - 1]))
+    first = f_part[vec_span(row), :]
+    for k in range(1, rows_n):
+        first = first + f_row[k - 1]
+    f_sub[sub] = first
+    landed(g_gather)
+    landed(sub_copies(1, f_sub))
+    first = f_sub[0]
+    for k in range(1, subs):
+        first = first + f_sub[k]
     second = first - dot_nn(first, g_full[...], HIGH)
-    coeffs = first + second
+    c_full[vec_span(row), :] = first + second
+    landed(row_copies(8, lambda peer: c_full.at[vec_span(row)], lambda k: c_full.at[vec_span(row)]))
+    coeffs = c_full[...]
     twice = block_t - dot_nn(coeffs, vpad[...], HIGH)
     gram = dot_nt(twice, twice, HIGH)
     fold = 128 // vecs
     tall = vecs // fold
     packed = jnp.concatenate([gram[i * tall : (i + 1) * tall] for i in range(fold)], axis=1)
-    coef_ref[...] = coeffs.T[:nb]
-    packed = sum_all(packed, 2, 7, c_row, c_sub) * (1.0 / total_rows)
-    gram = jnp.concatenate([packed[:, i * vecs : (i + 1) * vecs] for i in range(fold)], axis=0)
-    upper, inverse = factor_gram(gram, vecs)
-    rfac_ref[...] = upper
-    q_ref[...] = dot_nn(inverse, twice, HIGH)
+    twice_ref[...] = twice
+    coef_ref[...] = coeffs
+    gram_ref[...] = sum_all(packed, 2, 7, c_row, c_sub) * (1.0 / total_rows)
 
     for copy in started:
         copy.wait_send()
@@ -409,7 +434,20 @@
     near_finish(True, back_up)
 
 
+def finish(packed_ref, twice_ref, coef_in, coef_ref, rfac_ref, q_ref):
+    vecs = twice_ref.shape[0]
+    packed = packed_ref[...]
+    gram = jnp.concatenate(
+        [packed[:, i : i + vecs] for i in range(0, packed.shape[1], vecs)], axis=0
+    )
+    coef_ref[...] = coef_in[:, : coef_ref.shape[1]]
+    upper, inverse = factor_gram(gram, vecs)
+    rfac_ref[...] = upper
+    q_ref[:, 0, :] = dot_nn(inverse, twice_ref[...], HIGH)
+
+
 def per_device(residual, factor, basis, send_rows):
+    arrays = (residual, factor, basis, send_rows)
     subs = lax.axis_size("sub")
     rows_n = lax.axis_size("row")
     vecs, _, slab = residual.shape
@@ -421,16 +459,20 @@
     g_rows = nb // rows_n
     fold = 128 // vecs
     vmem = pl.BlockSpec(memory_space=pltpu.VMEM)
-    coeffs, rfactor, block_q = pl.pallas_call(
+    hbm = pl.BlockSpec(memory_space=pltpu.HBM)
+    coeffs, packed, twice = pl.pallas_call(
         functools.partial(kernel, subs, rows_n),
         out_shape=(
-            jax.ShapeDtypeStruct((nb, vecs), F32),
-            jax.ShapeDtypeStruct((vecs, vecs), F32),
+            jax.ShapeDtypeStruct((vecs, pad), F32),
+            jax.ShapeDtypeStruct((vecs // fold, 128), F32),
             jax.ShapeDtypeStruct((vecs, slab), F32),
         ),
-        in_specs=[vmem, pl.BlockSpec(memory_space=pl.ANY), vmem, vmem],
+        in_specs=[hbm, hbm, hbm, hbm],
         out_specs=(vmem, vmem, vmem),
         scratch_shapes=[
+            pltpu.VMEM((vecs, 1, slab), F32),
+            pltpu.VMEM((nb, 1, slab), F32),
+            pltpu.VMEM((2, margin), jnp.int32),
             pltpu.VMEM((share, wide), F32),
             pltpu.VMEM((share, wide), BF16),
             pltpu.VMEM((share, wide), BF16),
@@ -449,13 +491,16 @@
             pltpu.VMEM((rows_n - 1, g_rows, pad), F32),
             pltpu.VMEM((subs, g_rows, pad), F32),
             pltpu.VMEM((pad, pad), F32),
-            pltpu.VMEM((rows_n, vecs, pad), F32),
-            pltpu.VMEM((subs, vecs, pad), F32),
+            pltpu.VMEM((rows_n - 1, vecs // rows_n, pad), F32),
+            pltpu.VMEM((subs, vecs // rows_n, pad), F32),
             pltpu.VMEM((rows_n, vecs // fold, 128), F32),
             pltpu.VMEM((subs, vecs // fold, 128), F32),
+            pltpu.VMEM((vecs, pad), F32),
+            pltpu.VMEM((vecs, pad), F32),
+            pltpu.SemaphoreType.DMA((3,)),
             pltpu.SemaphoreType.DMA((LOADS,)),
-            pltpu.SemaphoreType.DMA((8, rows_n - 1)),
-            pltpu.SemaphoreType.DMA((8, rows_n - 1)),
+            pltpu.SemaphoreType.DMA((9, rows_n - 1)),
+            pltpu.SemaphoreType.DMA((9, rows_n - 1)),
             pltpu.SemaphoreType.DMA((4, rows_n)),
             pltpu.SemaphoreType.DMA((4, rows_n)),
             pltpu.SemaphoreType.DMA((3, subs - 1)),
@@ -467,8 +512,18 @@
         cost_estimate=pl.CostEstimate(
             flops=12 * vecs * share * wide, bytes_accessed=4 * share * wide, transcendentals=0
         ),
-    )(residual[:, 0, :], factor[0], basis[:, 0, :], send_rows[0])
-    return coeffs, rfactor, block_q[:, None, :]
+    )(*(pltpu.with_memory_space_constraint(array, pltpu.HBM) for array in arrays))
+    coeffs, rfactor, block_q = pl.pallas_call(
+        finish,
+        out_shape=(
+            jax.ShapeDtypeStruct((vecs, nb), F32),
+            jax.ShapeDtypeStruct((vecs, vecs), F32),
+            jax.ShapeDtypeStruct((vecs, 1, slab), F32),
+        ),
+        in_specs=[vmem, vmem, vmem],
+        out_specs=(vmem, vmem, vmem),
+    )(packed, twice, coeffs)
+    return coeffs.T, rfactor, block_q
 
 
 def solution(mesh):

time: 57.1 us -> 51.3 us (0.90)
  local copies, waits for them, and re-layouts: 8.13 us -> 1.79 us
  Pallas kernels: 48 us -> 48.7 us
    unnamed x9 -> x6, local copies, waits for them, and re-layouts: 8.13 us -> 1.79 us
    pallas_call x0 -> x1, Pallas kernels: none -> 4.39 us  [per_device(): pl.pallas_call(finish, out_shape=(jax.ShapeDtypeStruct((vecs, nb), F32),...]
    pallas_call x1, Pallas kernels: 48 us -> 44.3 us  [per_device(): pl.pallas_call(functools.partial(kernel, subs, rows_n), out_shape=(jax.Sh...]
where the time goes in v2:
time: 51.3 us; the launch traced here: 51.2 us
  Pallas kernels  48.7 us (95%)
  local copies, waits for them, and re-layouts  1.79 us (3%)
  between operations  0.65 us (1%)
    pallas_call x1, Pallas kernels, per_device(): pl.pallas_call(functools.partial(kernel, subs, rows_n), out_shape=(jax.Sh...  44.3 us
    pallas_call x1, Pallas kernels, per_device(): pl.pallas_call(finish, out_shape=(jax.ShapeDtypeStruct((vecs, nb), F32),...  4.39 us
    unnamed x6, local copies, waits for them, and re-layouts  1.79 us

profile of v2, /device:TPU:0, one launch (start us, length us, event | category | flops | bytes accessed | tf_op | source)
XLA Modules:
  0.0 51.2 jit_solution(11762637888003334905)
XLA Ops:
  0.6 44.3 %shard_map.67 = (f32[32,128]{1,0:T(8,128)S(1)}, f32[8,128]{1,0:T(8,128)S(1)}, f32[32,512]{1,0:T(8,128)S(1)}) custom-call(f32[32,1,512]{2,1,0:T(1,128)} %res_hbm.1, f32[1,768,3072]{2,1,0:T(8,128)} %fac_hbm.1, f32[96,1,512]{2,1,0:T(1,128)} %bas_hbm.1, s32[1,2,512]{2,1,0:T(2,128)} %idx_hbm.1), custom_call_target="tpu_custom_call" | custom-call | flops 905969664 | bytes 9437184 | tf_op jit(solution)/shard_map/pallas_call | solution.py:463
  45.0 0.0 copy-start
  45.0 0.6 %copy-done = f32[32,512]{1,0:T(8,128)} copy-done((f32[32,512]{1,0:T(8,128)}, f32[32,512]{1,0:T(8,128)S(1)}, u32[]{:S(2)}) %copy-start) | copy-done | bytes 65560
  45.6 0.0 copy-start.1
  45.6 0.6 %copy-done.1 = f32[32,128]{1,0:T(8,128)} copy-done((f32[32,128]{1,0:T(8,128)}, f32[32,128]{1,0:T(8,128)S(1)}, u32[]{:S(2)}) %copy-start.1) | copy-done | bytes 16408
  46.2 0.0 copy-start.2
  46.2 0.6 %copy-done.2 = f32[8,128]{1,0:T(8,128)} copy-done((f32[8,128]{1,0:T(8,128)}, f32[8,128]{1,0:T(8,128)S(1)}, u32[]{:S(2)}) %copy-start.2) | copy-done | bytes 4120
  46.8 4.4 %shard_map.68 = (f32[32,96]{1,0:T(8,128)}, f32[32,32]{1,0:T(8,128)}, f32[32,1,512]{2,1,0:T(1,128)}) custom-call(f32[8,128]{1,0:T(8,128)} %copy-done.2, f32[32,512]{1,0:T(8,128)} %copy-done, f32[32,128]{1,0:T(8,128)} %copy-done.1), custom_call_target="tpu_custom_call" | custom-call | tf_op jit(solution)/shard_map/pallas_call | solution.py:516
Async XLA Ops:
  45.0 0.6 %copy-start = (f32[32,512]{1,0:T(8,128)}, f32[32,512]{1,0:T(8,128)S(1)}, u32[]{:S(2)}) copy-start(f32[32,512]{1,0:T(8,128)S(1)} %get-tuple-element.10.twice_ref) | copy-start | bytes 196612
  45.6 0.6 %copy-start.1 = (f32[32,128]{1,0:T(8,128)}, f32[32,128]{1,0:T(8,128)S(1)}, u32[]{:S(2)}) copy-start(f32[32,128]{1,0:T(8,128)S(1)} %get-tuple-element.11.coef_in) | copy-start | bytes 49156
  46.2 0.6 %copy-start.2 = (f32[8,128]{1,0:T(8,128)}, f32[8,128]{1,0:T(8,128)S(1)}, u32[]{:S(2)}) copy-start(f32[8,128]{1,0:T(8,128)S(1)} %get-tuple-element.9.packed_ref) | copy-start | bytes 12292

commit v3 on v2

--- a/solution.py
+++ b/solution.py
@@ -44,12 +44,21 @@
         == lax.broadcasted_iota(jnp.int32, (vecs, vecs), 1)
     ).astype(F32)
     work = jnp.concatenate([gram, eye, jnp.zeros((vecs, 128 - 2 * vecs), F32)], axis=1)
-    row_of = lax.broadcasted_iota(jnp.int32, (vecs, 1), 0)
-    for step in range(vecs - 1):
-        scale = 1.0 / work[step : step + 1, step : step + 1]
-        multiplier = jnp.where(row_of > step, work[:, step : step + 1] * scale, 0.0)
-        work = work - multiplier * work[step : step + 1, :]
     rows = lax.broadcasted_iota(jnp.int32, work.shape, 0)
+    block = 8
+    for start in range(0, vecs, block):
+        spread = [
+            jnp.broadcast_to(work[:, at : at + 1], work.shape) for at in range(start, start + block)
+        ]
+        for j in range(block):
+            at = start + j
+            if at == vecs - 1:
+                break
+            scale = 1.0 / spread[j][at : at + 1, :]
+            multiplier = jnp.where(rows > at, spread[j] * scale, 0.0)
+            for later in range(j + 1, block):
+                spread[later] = spread[later] - multiplier * spread[later][at : at + 1, :]
+            work = work - multiplier * work[at : at + 1, :]
     lanes = lax.broadcasted_iota(jnp.int32, work.shape, 1)
     pivots = jnp.sum(jnp.where(rows == lanes, work, 0.0), axis=1, keepdims=True)
     work = jnp.where(lanes >= rows, work, 0.0) * (1.0 / jnp.sqrt(pivots))
@@ -522,6 +531,7 @@
         ),
         in_specs=[vmem, vmem, vmem],
         out_specs=(vmem, vmem, vmem),
+        compiler_params=pltpu.CompilerParams(vmem_limit_bytes=8 * 1024 * 1024),
     )(packed, twice, coeffs)
     return coeffs.T, rfactor, block_q
 

time: 51.3 us -> 46.9 us (0.914)
  Pallas kernels: 48.7 us -> 46.1 us
  local copies, waits for them, and re-layouts: 1.79 us -> 0 us
    pallas_call x1, Pallas kernels: 4.39 us -> 1.81 us  [per_device(): pl.pallas_call(finish, out_shape=(jax.ShapeDtypeStruct((vecs, nb), F32),...]
    unnamed x6 -> x0, local copies, waits for them, and re-layouts: 1.79 us -> none
where the time goes in v3:
time: 46.9 us; the launch traced here: 46.8 us
  Pallas kernels  46.1 us (98%)
  between operations  0.64 us (1%)
    pallas_call x1, Pallas kernels, per_device(): pl.pallas_call(functools.partial(kernel, subs, rows_n), out_shape=(jax.Sh...  44.3 us
    pallas_call x1, Pallas kernels, per_device(): pl.pallas_call(finish, out_shape=(jax.ShapeDtypeStruct((vecs, nb), F32),...  1.81 us

profile of v3, /device:TPU:0, one launch (start us, length us, event | category | flops | bytes accessed | tf_op | source)
XLA Modules:
  0.0 46.8 jit_solution(11794802446966229272)
XLA Ops:
  0.6 44.3 %shard_map.67 = (f32[32,128]{1,0:T(8,128)S(1)}, f32[8,128]{1,0:T(8,128)S(1)}, f32[32,512]{1,0:T(8,128)S(1)}) custom-call(f32[32,1,512]{2,1,0:T(1,128)} %res_hbm.1, f32[1,768,3072]{2,1,0:T(8,128)} %fac_hbm.1, f32[96,1,512]{2,1,0:T(1,128)} %bas_hbm.1, s32[1,2,512]{2,1,0:T(2,128)} %idx_hbm.1), custom_call_target="tpu_custom_call" | custom-call | flops 905969664 | bytes 9437184 | tf_op jit(solution)/shard_map/pallas_call | solution.py:472
  45.0 1.8 %shard_map.68 = (f32[32,96]{1,0:T(8,128)}, f32[32,32]{1,0:T(8,128)}, f32[32,1,512]{2,1,0:T(1,128)}) custom-call(f32[8,128]{1,0:T(8,128)S(1)} %get-tuple-element.9.packed_ref, f32[32,512]{1,0:T(8,128)S(1)} %get-tuple-element.10.twice_ref, f32[32,128]{1,0:T(8,128)S(1)} %get-tuple-element.11.coef_in), custom_call_target="tpu_custom_call" | custom-call | tf_op jit(solution)/shard_map/pallas_call | solution.py:525

commit v4 on v3

--- a/solution.py
+++ b/solution.py
@@ -102,6 +102,10 @@
     c_sub,
     f_part,
     c_full,
+    v_part,
+    v_rs,
+    v_quarter,
+    v_mar,
     small_sem,
     load_sem,
     row_send,
@@ -206,7 +210,7 @@
         started.extend(copies)
         return copies
 
-    def near_copies(slot, up, source, target):
+    def near_copies(slot, up, source, target, count=rows_n):
         to_sub = sub + 1 if up else sub - 1
         return [
             pltpu.make_async_remote_copy(
@@ -217,7 +221,7 @@
                 device_id=(to_sub, row_peer(k)),
                 device_id_type=MESH,
             )
-            for k in range(rows_n)
+            for k in range(count)
         ]
 
     def near_start(up, copies):
@@ -253,6 +257,16 @@
     small[2].wait()
     vpad[:nb] = bas_ref[:, 0, :]
     vpad[nb:] = jnp.zeros((vpad.shape[0] - nb, slab), F32)
+    my_rows = row * slab + lax.broadcasted_iota(jnp.int32, (slab, margin), 0)
+    hot[:, :margin] = (my_rows == idx_ref[1:2, :]).astype(F32).astype(BF16)
+    hot[:, margin:] = (my_rows == idx_ref[0:1, :]).astype(F32).astype(BF16)
+    g_part[...] = dot_nt(vpad[...], vpad[...], HIGH)
+    picked = dot_nn(jnp.concatenate(split_three(vpad[:nb]), axis=0), hot[...])
+    picked = picked[:nb] + picked[nb : 2 * nb] + picked[2 * nb :]
+    for which in range(rows_n):
+        for side in range(2):
+            at = side * margin + which * quarter
+            v_part[which, side] = picked[:, at : at + quarter]
     landed(slab_copies)
     whole = ext[:, :own]
     pieces = jnp.concatenate(split_three(whole), axis=0)
@@ -277,12 +291,12 @@
     def _():
         ext[:, own + margin :] = jnp.zeros((vecs, margin), F32)
 
-    g_part[...] = dot_nt(vpad[...], vpad[...], HIGH)
     g_rows = nb // rows_n
 
     def g_span(which):
         return pl.ds(pl.multiple_of(which * g_rows, 8), g_rows)
 
+    v_copies = row_copies(9, lambda peer: v_part.at[peer], lambda k: v_rs.at[k - 1])
     g_copies = row_copies(1, lambda peer: g_part.at[g_span(peer)], lambda k: g_rs.at[k - 1])
 
     for i in range(LOADS):
@@ -312,6 +326,27 @@
     for k in range(1, rows_n):
         g_mine = g_mine + g_rs[k - 1]
     g_sub[sub] = g_mine
+    landed(v_copies)
+    for side in range(2):
+        total = v_part[row, side]
+        for k in range(1, rows_n):
+            total = total + v_rs[k - 1, side]
+        v_quarter[side] = total
+    v_up = near_copies(4, True, v_quarter.at[0], v_mar.at[0, :nb], 1)
+    v_down = near_copies(5, False, v_quarter.at[1], v_mar.at[1, :nb], 1)
+    near_start(True, v_up)
+    near_start(False, v_down)
+    for side in range(2):
+        v_mar[side, nb:, :] = jnp.zeros((v_mar.shape[1] - nb, quarter), F32)
+
+    @pl.when(jnp.logical_not(has_lower))
+    def _():
+        v_mar[0, :nb, :] = jnp.zeros((nb, quarter), F32)
+
+    @pl.when(jnp.logical_not(has_upper))
+    def _():
+        v_mar[1, :nb, :] = jnp.zeros((nb, quarter), F32)
+
     g_across = sub_copies(0, g_sub)
 
     near_wait(True, up_copies)
@@ -381,18 +416,10 @@
     def _():
         back[:, margin:] = jnp.zeros((vecs, margin), F32)
 
-    my_rows = row * slab + lax.broadcasted_iota(jnp.int32, (slab, margin), 0)
-    hot[:, :margin] = (my_rows == idx_ref[1:2, :]).astype(F32).astype(BF16)
-    hot[:, margin:] = (my_rows == idx_ref[0:1, :]).astype(F32).astype(BF16)
     landed(own_copies)
     block_t = own_of(row)[...]
     for k in range(1, rows_n):
         block_t = block_t + rs_own[k - 1]
-    near_wait(False, back_down)
-    near_wait(True, back_up)
-    added = dot_nt(jnp.concatenate(split_three(back[...]), axis=0), hot[...])
-    block_t = block_t + (added[:vecs] + added[vecs : 2 * vecs] + added[2 * vecs :])
-
     def sum_all(value, slot, row_slot, by_row, by_sub):
         by_row[row] = value
         landed(row_copies(row_slot, lambda peer: by_row.at[row], lambda k: by_row.at[row]))
@@ -411,14 +438,25 @@
     def vec_span(which):
         return pl.ds(pl.multiple_of(which * eighth, 8), eighth)
 
-    f_part[...] = dot_nt(block_t, vpad[...], HIGH)
+    near_wait(True, v_up)
+    near_wait(False, v_down)
+    f_part[...] = (
+        dot_nt(block_t, vpad[...], HIGH)
+        + dot_nt(back_q[0], v_mar[0], HIGH)
+        + dot_nt(back_q[1], v_mar[1], HIGH)
+    )
     landed(row_copies(6, lambda peer: f_part.at[vec_span(peer)], lambda k: f_row.at[k - 1]))
     first = f_part[vec_span(row), :]
     for k in range(1, rows_n):
         first = first + f_row[k - 1]
     f_sub[sub] = first
+    f_across = sub_copies(1, f_sub)
+    near_wait(False, back_down)
+    near_wait(True, back_up)
+    added = dot_nt(jnp.concatenate(split_three(back[...]), axis=0), hot[...])
+    block_t = block_t + (added[:vecs] + added[vecs : 2 * vecs] + added[2 * vecs :])
     landed(g_gather)
-    landed(sub_copies(1, f_sub))
+    landed(f_across)
     first = f_sub[0]
     for k in range(1, subs):
         first = first + f_sub[k]
@@ -441,6 +479,8 @@
     near_finish(False, down_copies)
     near_finish(False, back_down)
     near_finish(True, back_up)
+    near_finish(True, v_up)
+    near_finish(False, v_down)
 
 
 def finish(packed_ref, twice_ref, coef_in, coef_ref, rfac_ref, q_ref):
@@ -506,12 +546,16 @@
             pltpu.VMEM((subs, vecs // fold, 128), F32),
             pltpu.VMEM((vecs, pad), F32),
             pltpu.VMEM((vecs, pad), F32),
+            pltpu.VMEM((rows_n, 2, nb, quarter), F32),
+            pltpu.VMEM((rows_n - 1, 2, nb, quarter), F32),
+            pltpu.VMEM((2, nb, quarter), F32),
+            pltpu.VMEM((2, pad, quarter), F32),
             pltpu.SemaphoreType.DMA((3,)),
             pltpu.SemaphoreType.DMA((LOADS,)),
-            pltpu.SemaphoreType.DMA((9, rows_n - 1)),
-            pltpu.SemaphoreType.DMA((9, rows_n - 1)),
-            pltpu.SemaphoreType.DMA((4, rows_n)),
-            pltpu.SemaphoreType.DMA((4, rows_n)),
+            pltpu.SemaphoreType.DMA((10, rows_n - 1)),
+            pltpu.SemaphoreType.DMA((10, rows_n - 1)),
+            pltpu.SemaphoreType.DMA((6, rows_n)),
+            pltpu.SemaphoreType.DMA((6, rows_n)),
             pltpu.SemaphoreType.DMA((3, subs - 1)),
             pltpu.SemaphoreType.DMA((3, subs - 1)),
         ],

time: 46.9 us -> 47.7 us (1.017)
  Pallas kernels: 46.1 us -> 46.9 us
    pallas_call x1, Pallas kernels: 44.3 us -> 45.1 us  [per_device(): pl.pallas_call(functools.partial(kernel, subs, rows_n), out_shape=(jax.Sh...]
where the time goes in v4:
time: 47.7 us; the launch traced here: 47.5 us
  Pallas kernels  46.9 us (98%)
  between operations  0.64 us (1%)
    pallas_call x1, Pallas kernels, per_device(): pl.pallas_call(functools.partial(kernel, subs, rows_n), out_shape=(jax.Sh...  45.1 us
    pallas_call x1, Pallas kernels, per_device(): pl.pallas_call(finish, out_shape=(jax.ShapeDtypeStruct((vecs, nb), F32),...  1.81 us

profile of v4, /device:TPU:0, one launch (start us, length us, event | category | flops | bytes accessed | tf_op | source)
XLA Modules:
  0.0 47.5 jit_solution(7853054547703055965)
XLA Ops:
  0.6 45.1 %shard_map.67 = (f32[32,128]{1,0:T(8,128)S(1)}, f32[8,128]{1,0:T(8,128)S(1)}, f32[32,512]{1,0:T(8,128)S(1)}) custom-call(f32[32,1,512]{2,1,0:T(1,128)} %res_hbm.1, f32[1,768,3072]{2,1,0:T(8,128)} %fac_hbm.1, f32[96,1,512]{2,1,0:T(1,128)} %bas_hbm.1, s32[1,2,512]{2,1,0:T(2,128)} %idx_hbm.1), custom_call_target="tpu_custom_call" | custom-call | flops 905969664 | bytes 9437184 | tf_op jit(solution)/shard_map/pallas_call | solution.py:512
  45.7 1.8 %shard_map.68 = (f32[32,96]{1,0:T(8,128)}, f32[32,32]{1,0:T(8,128)}, f32[32,1,512]{2,1,0:T(1,128)}) custom-call(f32[8,128]{1,0:T(8,128)S(1)} %get-tuple-element.9.packed_ref, f32[32,512]{1,0:T(8,128)S(1)} %get-tuple-element.10.twice_ref, f32[32,128]{1,0:T(8,128)S(1)} %get-tuple-element.11.coef_in), custom_call_target="tpu_custom_call" | custom-call | tf_op jit(solution)/shard_map/pallas_call | solution.py:569

commit v5 on v3

--- a/solution.py
+++ b/solution.py
@@ -253,6 +253,19 @@
     small[2].wait()
     vpad[:nb] = bas_ref[:, 0, :]
     vpad[nb:] = jnp.zeros((vpad.shape[0] - nb, slab), F32)
+    g_part[...] = dot_nt(vpad[...], vpad[...], HIGH)
+    def split_loads(first, last):
+        for i in range(first, last):
+            loads[i].wait()
+
+            @pl.loop(0, load_rows // 16)
+            def _(j):
+                span = pl.ds(pl.multiple_of(i * load_rows + j * 16, 16), 16)
+                high, low = split_two(fac[span, :])
+                fhi[span, :] = high
+                flo[span, :] = low
+
+    split_loads(0, LOADS // 2)
     landed(slab_copies)
     whole = ext[:, :own]
     pieces = jnp.concatenate(split_three(whole), axis=0)
@@ -277,7 +290,6 @@
     def _():
         ext[:, own + margin :] = jnp.zeros((vecs, margin), F32)
 
-    g_part[...] = dot_nt(vpad[...], vpad[...], HIGH)
     g_rows = nb // rows_n
 
     def g_span(which):
@@ -285,15 +297,7 @@
 
     g_copies = row_copies(1, lambda peer: g_part.at[g_span(peer)], lambda k: g_rs.at[k - 1])
 
-    for i in range(LOADS):
-        loads[i].wait()
-
-        @pl.loop(0, load_rows // 16)
-        def _(j):
-            span = pl.ds(pl.multiple_of(i * load_rows + j * 16, 16), 16)
-            high, low = split_two(fac[span, :])
-            fhi[span, :] = high
-            flo[span, :] = low
+    split_loads(LOADS // 2, LOADS)
 
     high, low = split_two(whole)
     stack[:vecs, :own] = high

time: 46.9 us -> 46.9 us (level)
  no operation moved by 1% of the time
where the time goes in v5:
time: 46.9 us; the launch traced here: 46.7 us
  Pallas kernels  46.1 us (98%)
  between operations  0.64 us (1%)
    pallas_call x1, Pallas kernels, per_device(): pl.pallas_call(functools.partial(kernel, subs, rows_n), out_shape=(jax.Sh...  44.3 us
    pallas_call x1, Pallas kernels, per_device(): pl.pallas_call(finish, out_shape=(jax.ShapeDtypeStruct((vecs, nb), F32),...  1.81 us

profile of v5, /device:TPU:0, one launch (start us, length us, event | category | flops | bytes accessed | tf_op | source)
XLA Modules:
  0.0 46.7 jit_solution(8798440297772952923)
XLA Ops:
  0.6 44.3 %shard_map.67 = (f32[32,128]{1,0:T(8,128)S(1)}, f32[8,128]{1,0:T(8,128)S(1)}, f32[32,512]{1,0:T(8,128)S(1)}) custom-call(f32[32,1,512]{2,1,0:T(1,128)} %res_hbm.1, f32[1,768,3072]{2,1,0:T(8,128)} %fac_hbm.1, f32[96,1,512]{2,1,0:T(1,128)} %bas_hbm.1, s32[1,2,512]{2,1,0:T(2,128)} %idx_hbm.1), custom_call_target="tpu_custom_call" | custom-call | flops 905969664 | bytes 9437184 | tf_op jit(solution)/shard_map/pallas_call | solution.py:476
  44.9 1.8 %shard_map.68 = (f32[32,96]{1,0:T(8,128)}, f32[32,32]{1,0:T(8,128)}, f32[32,1,512]{2,1,0:T(1,128)}) custom-call(f32[8,128]{1,0:T(8,128)S(1)} %get-tuple-element.9.packed_ref, f32[32,512]{1,0:T(8,128)S(1)} %get-tuple-element.10.twice_ref, f32[32,128]{1,0:T(8,128)S(1)} %get-tuple-element.11.coef_in), custom_call_target="tpu_custom_call" | custom-call | tf_op jit(solution)/shard_map/pallas_call | solution.py:529
